TPU v7x, 32 devices: a whole 2x2x4 slice. The times are simulated.
32 devices in a mesh: parts: 2 (over y), dp: 4 (over z), tensor: 4 (over x, core).
Axes of the slice: x: 2, y: 2, z: 4, core: 2. Of those that a mesh axis runs over, the one named last changes fastest.
Arguments:
- queries: bfloat16 [256, 64, 128], P(('parts', 'dp'), 'tensor'), parts along dimension 0, may hold values from -4 to 4
- cache_keys: bfloat16 [256, 8, 128, 128], P(('parts', 'dp'), 'tensor'), parts along dimension 0, may hold values from -8 to 8
- cache_values: bfloat16 [256, 8, 128, 128], P(('parts', 'dp'), 'tensor'), parts along dimension 0, may hold values from -6 to 6
- new_key: bfloat16 [256, 8, 128], P(('parts', 'dp'), 'tensor'), parts along dimension 0, may hold values from -8 to 8
- new_value: bfloat16 [256, 8, 128], P(('parts', 'dp'), 'tensor'), parts along dimension 0, may hold values from -6 to 6
- lengths: int32 [8, 32], P(('parts', 'dp')), parts along dimension 0, may hold values from 1 to 128, 2048 in all within a row
- adapter_ids: int32 [256], P(('parts', 'dp')), parts along dimension 0, may hold values from 0 to 31, as said below
- adapter_home: int32 [64], P('parts'), parts along dimension 0, may hold values from 0 to 31, as said below
- w_out: bfloat16 [8192, 4096], P('tensor'), may hold values from -0.0625 to 0.0625
- factor_a: bfloat16 [32, 64, 8192], P('dp', None, 'tensor'), may hold values from -0.0625 to 0.0625
- up_factor_table: bfloat16 [32, 64, 4096], P('dp', None, 'tensor'), may hold values from -0.75 to 0.75
Outputs:
- projected: bfloat16 [256, 4096], P(('parts', 'dp'), 'tensor'), parts along dimension 0
There are 2 independent parts, one for each index of `parts`. A program takes and returns all parts, laid end to end along the dimension named above; an argument that names none is the same for every part. Nothing has to cross between parts.
Inputs may be any that keep to these rules, and one draw needn't show every extreme that they name: `adapter_ids`: the rows of one group name at most 2 different adapters whose storage positions share the value position // 8; in every group some such value is shared by exactly 2 of them. `adapter_home`: A permutation. `lengths`: the 32 entries of one group (one line of the array) sum to 2048; in every group one row has exactly 128 cached positions.
All inputs are finite; a program needn't handle non-finite values.
Results may differ from a plain program's by a relative error of at most 0.008.
Values may be sent and summed in bfloat16 or wider, within the bound.
A program may use at most 128 MiB of HBM per device.

v0:
```python
import math

import jax
import jax.numpy as jnp
from jax import lax
from jax.sharding import PartitionSpec as P

SLOTS = 2


ADAPTER_SCALING = 2.0


def attend(queries, cache_keys, cache_values, new_key, new_value, lengths):
    row_count, head_count, head_width = queries.shape
    kv_count = cache_keys.shape[1]
    cache_span = cache_keys.shape[2]
    grouped = queries.reshape(row_count, kv_count, head_count // kv_count, head_width)
    score_scale = 1.0 / math.sqrt(head_width)
    scores = (
        jnp.einsum("rkgd,rkpd->rkgp", grouped, cache_keys, preferred_element_type=jnp.float32)
        * score_scale
    )
    own_score = (
        jnp.einsum("rkgd,rkd->rkg", grouped, new_key, preferred_element_type=jnp.float32)
        * score_scale
    )
    visible = jnp.arange(cache_span)[None, :] < lengths.reshape(row_count)[:, None]
    visible = visible[:, None, None, :]
    row_top = jnp.maximum(jnp.max(jnp.where(visible, scores, -jnp.inf), axis=-1), own_score)
    weights = jnp.where(visible, jnp.exp(scores - row_top[..., None]), 0.0)
    own_weight = jnp.exp(own_score - row_top)
    row_total = jnp.sum(weights, axis=-1) + own_weight
    probs = (weights / row_total[..., None]).astype(jnp.bfloat16)
    own_prob = (own_weight / row_total).astype(jnp.bfloat16)
    mixed = jnp.einsum("rkgp,rkpd->rkgd", probs, cache_values, preferred_element_type=jnp.float32)
    mixed = (
        mixed
        + own_prob.astype(jnp.float32)[..., None] * new_value.astype(jnp.float32)[:, :, None, :]
    )
    return mixed.astype(jnp.bfloat16).reshape(row_count, head_count * head_width)


def lookup(indices, table):
    match = indices[:, None] == jnp.arange(table.shape[0], dtype=jnp.int32)[None, :]
    return jnp.sum(jnp.where(match, table[None, :], 0), axis=1)


def local(
    queries,
    cache_keys,
    cache_values,
    new_key,
    new_value,
    lengths,
    adapter_ids,
    adapter_home,
    w_out,
    factor_a,
    up_factor_table,
):
    attended = attend(queries, cache_keys, cache_values, new_key, new_value, lengths)
    row_count = attended.shape[0]
    stored = factor_a.shape[0]
    adapter_rank_width = factor_a.shape[1]
    out_share = up_factor_table.shape[2]
    group_count = lax.axis_size("dp")
    adapter_total = adapter_home.shape[0]
    position = lookup(adapter_ids, adapter_home)
    owner_of = position // stored
    every_id = lax.all_gather(adapter_ids, "dp", axis=0, tiled=True)
    every_position = lookup(every_id, adapter_home)
    group_of = jnp.arange(group_count * row_count, dtype=jnp.int32) // row_count
    group_match = (group_of[None, :] == jnp.arange(group_count, dtype=jnp.int32)[:, None]).astype(
        jnp.bfloat16
    )
    slot_match = (
        every_position[:, None] == jnp.arange(adapter_total, dtype=jnp.int32)[None, :]
    ).astype(jnp.bfloat16)
    needed = jnp.dot(group_match, slot_match, preferred_element_type=jnp.float32) > 0.5
    needed = needed.reshape(group_count, group_count, stored).astype(jnp.int32)
    slot_rank = jnp.cumsum(needed, axis=2) - needed
    myself = lax.axis_index("dp")
    my_needed = lax.dynamic_index_in_dim(needed, myself, axis=1, keepdims=False)
    my_rank = lax.dynamic_index_in_dim(slot_rank, myself, axis=1, keepdims=False)
    slot_ids = jnp.arange(SLOTS, dtype=jnp.int32)
    select = (
        (my_needed[:, None, :] > 0) & (my_rank[:, None, :] == slot_ids[None, :, None])
    ).astype(jnp.bfloat16)
    packed_a = jnp.einsum(
        "gsl,lkj->gskj", select, factor_a, preferred_element_type=jnp.float32
    ).astype(jnp.bfloat16)
    packed_b = jnp.einsum(
        "gsl,lkj->gskj", select, up_factor_table, preferred_element_type=jnp.float32
    ).astype(jnp.bfloat16)
    arrived_a, received_up_factor = (
        lax.all_to_all(packed_a, "dp", split_axis=0, concat_axis=0, tiled=True),
        lax.all_to_all(packed_b, "dp", split_axis=0, concat_axis=0, tiled=True),
    )
    slot_total = group_count * SLOTS
    arrived_a = arrived_a.reshape(slot_total, adapter_rank_width, arrived_a.shape[3])
    received_up_factor = received_up_factor.reshape(slot_total * adapter_rank_width, out_share)
    rank_here = lax.dynamic_index_in_dim(slot_rank, myself, axis=0, keepdims=False).reshape(
        adapter_total
    )
    row_slot = owner_of * SLOTS + lookup(position, rank_here)
    one_hot = row_slot[:, None] == jnp.arange(slot_total, dtype=jnp.int32)[None, :]
    shrink_all = jnp.einsum("rj,skj->rsk", attended, arrived_a, preferred_element_type=jnp.float32)
    shrink_part = jnp.sum(jnp.where(one_hot[:, :, None], shrink_all, 0.0), axis=1)
    shrunk = lax.psum(shrink_part, "tensor").astype(jnp.bfloat16)
    slot_block_rows = jnp.where(
        one_hot[:, :, None], shrunk[:, None, :], jnp.zeros((), jnp.bfloat16)
    )
    slot_block_rows = slot_block_rows.reshape(row_count, slot_total * adapter_rank_width)
    adapter_delta = jnp.dot(slot_block_rows, received_up_factor, preferred_element_type=jnp.float32)
    base_output = jnp.dot(attended, w_out, preferred_element_type=jnp.float32)
    combined_output = lax.psum_scatter(base_output, "tensor", scatter_dimension=1, tiled=True)
    return (combined_output + ADAPTER_SCALING * adapter_delta).astype(jnp.bfloat16)


def solution(mesh):
    in_specs = (
        P(("parts", "dp"), "tensor", None),
        P(("parts", "dp"), "tensor", None, None),
        P(("parts", "dp"), "tensor", None, None),
        P(("parts", "dp"), "tensor", None),
        P(("parts", "dp"), "tensor", None),
        P(("parts", "dp"), None),
        P(("parts", "dp")),
        P("parts"),
        P("tensor", None),
        P("dp", None, "tensor"),
        P("dp", None, "tensor"),
    )
    out_specs = P(("parts", "dp"), "tensor")
    return jax.shard_map(local, mesh=mesh, in_specs=in_specs, out_specs=out_specs, check_vma=False)
```

profile of v0, /device:TPU:0, one launch (start us, length us, event | category | flops | bytes accessed | tf_op | source)
XLA Modules:
  0.0 123.1 jit_solution(8609628348734487561)
XLA Ops:
  6.5 1.4 %dynamic-slice = u32[1]{0:T(128)} dynamic-slice(u32[32]{0:T(128)} %constant.74, u32[]{:T(128)S(6)} %add.42), dynamic_slice_sizes={1} | dynamic-slice | bytes 12
  8.6 0.9 dynamic-update-slice
  9.4 9.9 %all-reduce = s32[128]{0:T(128)S(1)} all-reduce(s32[128]{0:T(128)S(1)} %dynamic-update-slice), channel_id=1, replica_groups=mesh['parts'=2,'dp'=4,'tensor'=4] {'dp'}, use_global_device_ids=true, to_apply=%add | all-reduce | flops 128 | bytes 1024
  19.3 0.7 select_reduce_fusion.2
  20.1 0.2 fusion.6
  20.3 0.1 reshape.118
  20.4 0.7 reduce_window_sum.11
  21.1 3.4 %convolution_convert_fusion = bf16[4,2,64,2048]{3,0,2,1:T(4,128)(2,1)S(1)} fusion(bf16[8,64,2048]{2,1,0:T(8,128)(2,1)} %param.20, s32[4,8]{1,0:T(4,128)S(1)} %bitcast.60, pred[4,8]{1,0:T(4,128)(4,1)S(1)} %bitcast.62), kind=kOutput, calls=%fused_computation | convolution fusion | flops 17825920 | bytes 4194464 | tf_op jit(solution)/shard_map/gsl,lkj->gskj/dot_general | solution.py:90
  24.5 2.4 %copy.43 = bf16[4,2,64,2048]{3,2,1,0:T(8,128)(2,1)} copy(bf16[4,2,64,2048]{3,0,2,1:T(4,128)(2,1)S(1)} %convolution_convert_fusion) | data formatting | bytes 4194304 | tf_op jit(solution)/shard_map/convert_element_type | solution.py:92
  27.0 4.6 %all-to-all-start = ((bf16[4,2,64,2048]{3,2,1,0:T(8,128)(2,1)}), bf16[4,2,64,2048]{3,2,1,0:T(8,128)(2,1)}, u32[]{:S(2)}, u32[]{:S(2)}) async-start(bf16[4,2,64,2048]{3,2,1,0:T(8,128)(2,1)} %copy.43), calls=%async_computation.1 | async-start | bytes 4194304 | tf_op jit(solution)/shard_map/all_to_all | solution.py:97
  31.6 0.6 convert_element_type.39
  32.3 2.2 %select_reduce_fusion = (f32[32,2,8]{2,1,0:T(2,128)S(1)}, f32[32,2,8,128]{3,2,1,0:T(8,128)S(1)}) fusion(pred[32,128]{1,0:T(8,128)(4,1)S(1)} %iota_compare_fusion.5, bf16[32,2,128,128]{3,2,1,0:T(8,128)(2,1)S(1)} %copy-done, bf16[32,16,128]{2,1,0:T(8,128)(2,1)} %param.11), kind=kOutput, calls=%fused_computation.18 | convolution fusion | flops 16973312 | bytes 2496512 | tf_op jit(solution)/shard_map/rkgd,rkpd->rkgp/dot_general | solution.py:21
  34.6 1.1 fusion.13
  35.8 0.1 copy.38
  35.9 0.3 fusion.9
  36.3 0.7 copy.41
  37.0 0.7 copy.40
  37.7 0.8 convolution_convert_fusion.1
  38.5 1.3 %copy.46 = bf16[4,2,64,1024]{3,2,1,0:T(8,128)(2,1)} copy(bf16[4,2,64,1024]{3,0,2,1:T(4,128)(2,1)S(1)} %convolution_convert_fusion.1) | data formatting | bytes 2097152 | tf_op jit(solution)/shard_map/convert_element_type | solution.py:95
  39.8 1.5 %fusion.2 = bf16[32,2,8,128]{3,2,1,0:T(8,128)(2,1)S(1)} fusion(bf16[32,2,128,128]{3,2,1,0:T(8,128)(2,1)S(1)} %copy-done.8, f32[32,2,8,128]{3,2,1,0:T(8,128)S(1)} %get-tuple-element.8, f32[32,2,128]{2,1,0:T(2,128)S(1)} %copy-done.5, f32[32,2,8]{2,1,0:T(2,128)S(1)} %copy-done.3, f32[32,2,8]{2,1,0:T(2,128)S(1)} %copy-done.4, f32[32,2,8]{2,1,0:T(2,128)} %copy-done.2, ...), kind=kOutput, calls=%fused_computation.6 | convolution fusion | flops 17235968 | bytes 2533376 | tf_op jit(solution)/shard_map/rkgp,rkpd->rkgd/dot_general | solution.py:36
  41.3 36.8 %all-to-all-done = bf16[4,2,64,2048]{3,2,1,0:T(8,128)(2,1)} async-done(((bf16[4,2,64,2048]{3,2,1,0:T(8,128)(2,1)}), bf16[4,2,64,2048]{3,2,1,0:T(8,128)(2,1)}, u32[]{:S(2)}, u32[]{:S(2)}) %all-to-all-start) | async-done | bytes 2097184 | tf_op jit(solution)/shard_map/all_to_all | solution.py:97
  78.1 3.5 %all-to-all-start.1 = ((bf16[4,2,64,1024]{3,2,1,0:T(8,128)(2,1)}), bf16[4,2,64,1024]{3,2,1,0:T(8,128)(2,1)S(1)}, u32[]{:S(2)}, u32[]{:S(2)}) async-start(bf16[4,2,64,1024]{3,2,1,0:T(8,128)(2,1)} %copy.46), calls=%async_computation.2 | async-start | bytes 2097152 | tf_op jit(solution)/shard_map/all_to_all | solution.py:98
  81.7 9.6 %fusion.10 = f32[32,4096]{1,0:T(8,128)} fusion(bf16[2048,4096]{1,0:T(8,128)(2,1)} %param.19, bf16[4,8,16,128]{3,2,1,0:T(8,128)(2,1)S(1)} %bitcast.59), kind=kOutput, calls=%fused_computation.20 | convolution fusion | flops 536870912 | bytes 17432576 | tf_op jit(solution)/shard_map/dot_general | solution.py:116
  91.3 0.2 select_reduce_fusion.3
  91.6 0.1 broadcast_in_dim.113
  91.6 0.2 select_reduce_fusion.1
  91.8 2.7 %fusion.5 = f32[32,64]{1,0:T(8,128)S(1)} fusion(bf16[32,2048,1]{1,0,2:T(8,128)(2,1)S(1)} %reshape.128, bf16[8,64,2048]{2,1,0:T(8,128)(2,1)} %bitcast.9, pred[32,8]{0,1:T(8,128)(4,1)S(1)} %iota_compare_fusion.7), kind=kOutput, calls=%fused_computation.11 | convolution fusion | flops 67139584 | bytes 2236672 | tf_op jit(solution)/shard_map/rj,skj->rsk/dot_general | solution.py:108
  94.5 10.4 %psum.7 = bf16[32,64]{1,0:T(8,128)(2,1)S(1)} all-reduce(f32[32,64]{1,0:T(8,128)S(1)} %fusion.5), channel_id=1, replica_groups=mesh['parts'=2,'dp'=4,'tensor'=4] {'tensor'}, use_global_device_ids=true, to_apply=%region_8.9 | all-reduce | flops 2048 | bytes 12288 | tf_op jit(solution)/shard_map/psum | solution.py:110
  105.0 0.1 broadcast_select_fusion
  105.1 0.1 select_n.71
  105.2 9.2 %reduce-scatter.2.cloned.1.call-done = f32[32,1024]{1,0:T(8,128)} async-done(((f32[32,4096]{1,0:T(8,128)}), f32[32,1024]{1,0:T(8,128)}) %reduce-scatter.2.cloned.1.call-update) | async-done | bytes 131088 | tf_op jit(solution)/shard_map/reduce_scatter | solution.py:117
  114.5 1.8 %fusion.4 = bf16[32,1024]{1,0:T(8,128)(2,1)} fusion(f32[32,1024]{1,0:T(8,128)} %reduce-scatter.2.cloned.1.call-done, bf16[32,512]{1,0:T(8,128)(2,1)S(1)} %select_n.71, bf16[512,1024]{1,0:T(8,128)(2,1)S(1)} %bitcast.58), kind=kOutput, calls=%fused_computation.10 | convolution fusion | flops 33652736 | bytes 1277952 | tf_op jit(solution)/shard_map/dot_general | solution.py:115
  (44 shorter events, 0.6 us)
Async XLA Ops:
  6.5 25.8 %copy-start = (bf16[32,2,128,128]{3,2,1,0:T(8,128)(2,1)S(1)}, bf16[32,2,128,128]{3,2,1,0:T(8,128)(2,1)}, u32[]{:S(2)}) copy-start(bf16[32,2,128,128]{3,2,1,0:T(8,128)(2,1)} %param.12) | copy-start | bytes 6291460
  27.0 4.6 %copy-start.6 = (bf16[32,2,128]{2,1,0:T(2,128)(2,1)S(1)}, bf16[32,2,128]{2,1,0:T(2,128)(2,1)}, u32[]{:S(2)}) copy-start(bf16[32,2,128]{2,1,0:T(2,128)(2,1)} %param.15) | copy-start | bytes 49156
  27.0 5.2 %copy-start.7 = (s32[1,32]{1,0:T(1,128)S(1)}, s32[1,32]{1,0:T(1,128)}, u32[]{:S(2)}) copy-start(s32[1,32]{1,0:T(1,128)} %param.16) | copy-start | bytes 388
  27.0 51.1 %all-to-all-start = ((bf16[4,2,64,2048]{3,2,1,0:T(8,128)(2,1)}), bf16[4,2,64,2048]{3,2,1,0:T(8,128)(2,1)}, u32[]{:S(2)}, u32[]{:S(2)}) async-start(bf16[4,2,64,2048]{3,2,1,0:T(8,128)(2,1)} %copy.43), calls=%async_computation.1 | async-start | bytes 4194304 | tf_op jit(solution)/shard_map/all_to_all | solution.py:97
  31.6 3.0 %copy-start.9 = (bf16[32,2,128]{2,1,0:T(2,128)(2,1)S(1)}, bf16[32,2,128]{2,1,0:T(2,128)(2,1)}, u32[]{:S(2)}) copy-start(bf16[32,2,128]{2,1,0:T(2,128)(2,1)} %param.14) | copy-start | bytes 49156
  31.6 6.1 %copy-start.1 = (bf16[8,64,1024]{2,1,0:T(8,128)(2,1)S(1)}, bf16[8,64,1024]{2,1,0:T(8,128)(2,1)}, u32[]{:S(2)}) copy-start(bf16[8,64,1024]{2,1,0:T(8,128)(2,1)} %param.21) | copy-start | bytes 3145732
  35.9 2.6 %copy-start.2 = (f32[32,2,8]{2,1,0:T(2,128)}, f32[32,2,8]{2,1,0:T(2,128)S(1)}, u32[]{:S(2)}) copy-start(f32[32,2,8]{2,1,0:T(2,128)S(1)} %copy.38) | copy-start | bytes 6148
  37.7 2.2 %copy-start.3 = (f32[32,2,8]{2,1,0:T(2,128)S(1)}, f32[32,2,8]{2,1,0:T(2,128)}, u32[]{:S(2)}) copy-start(f32[32,2,8]{2,1,0:T(2,128)} %copy.41) | copy-start | bytes 6148
  37.7 2.2 %copy-start.4 = (f32[32,2,8]{2,1,0:T(2,128)S(1)}, f32[32,2,8]{2,1,0:T(2,128)}, u32[]{:S(2)}) copy-start(f32[32,2,8]{2,1,0:T(2,128)} %copy.40) | copy-start | bytes 6148
  37.7 2.2 %copy-start.5 = (f32[32,2,128]{2,1,0:T(2,128)S(1)}, f32[32,2,128]{2,1,0:T(2,128)}, u32[]{:S(2)}) copy-start(f32[32,2,128]{2,1,0:T(2,128)} %convert_element_type.39) | copy-start | bytes 98308
  37.7 2.2 %copy-start.8 = (bf16[32,2,128,128]{3,2,1,0:T(8,128)(2,1)S(1)}, bf16[32,2,128,128]{3,2,1,0:T(8,128)(2,1)}, u32[]{:S(2)}) copy-start(bf16[32,2,128,128]{3,2,1,0:T(8,128)(2,1)} %param.13) | copy-start | bytes 6291460
  78.1 36.4 %all-to-all-start.1 = ((bf16[4,2,64,1024]{3,2,1,0:T(8,128)(2,1)}), bf16[4,2,64,1024]{3,2,1,0:T(8,128)(2,1)S(1)}, u32[]{:S(2)}, u32[]{:S(2)}) async-start(bf16[4,2,64,1024]{3,2,1,0:T(8,128)(2,1)} %copy.46), calls=%async_computation.2 | async-start | bytes 2097152 | tf_op jit(solution)/shard_map/all_to_all | solution.py:98
  81.6 32.9 %reduce-scatter.2.cloned.1.call-start = ((), (), s32[]{:S(2)}) async-start(), calls=%async_computation.3 | async-start | bytes 655360 | tf_op jit(solution)/shard_map/reduce_scatter | solution.py:117
  81.7 9.6 %copy-start.10 = (s32[32]{0:T(128)S(1)}, s32[32]{0:T(128)}, u32[]{:S(2)}) copy-start(s32[32]{0:T(128)} %param.18) | copy-start | bytes 388
  81.7 9.6 %copy-start.11 = (s32[32]{0:T(128)S(1)}, s32[32]{0:T(128)}, u32[]{:S(2)}) copy-start(s32[32]{0:T(128)} %param.17) | copy-start | bytes 388
Sparse Core Ops, SparseCore 0:
  91.4 23.0 reduce-scatter.1
where the time goes:
time: 124 us; the launch traced here: 123 us
  waiting for transfers between devices  46 us (37%)
  matrix products  23.3 us (19%)
  blocking collectives  20.3 us (16%)
  between operations  14.3 us (12%)
  local copies, waits for them, and re-layouts  8.13 us (7%)
  starting transfers between devices  8.13 us (7%)
  other arithmetic  2.95 us (2%)
    all_to_all x1, waiting for transfers between devices, local(): lax.all_to_all(packed_a, 'dp', split_axis=0, concat_axis=0, tiled=True)  36.8 us
    psum x1, blocking collectives, local(): shrunk = lax.psum(shrink_part, 'tensor').astype(jnp.bfloat16)  10.4 us
    unnamed x1, blocking collectives  9.89 us
    dot_general x1, matrix products, local(): base_output = jnp.dot(attended, w_out, preferred_element_type=jnp.float32)  9.56 us
    reduce_scatter x1, waiting for transfers between devices, local(): lax.psum_scatter(base_output, 'tensor', scatter_dimension=1, tiled=True)  9.23 us
    all_to_all x1, starting transfers between devices, local(): lax.all_to_all(packed_a, 'dp', split_axis=0, concat_axis=0, tiled=True)  4.57 us
    all_to_all x1, starting transfers between devices, local(): lax.all_to_all(packed_b, 'dp', split_axis=0, concat_axis=0, tiled=True)  3.52 us
    dot_general x1, matrix products, local(): jnp.einsum('gsl,lkj->gskj', select, factor_a, preferred_element_type=jnp....  3.4 us
  transfers between devices with their start and end apart: 3, of which 2 were waited for; matrix products, arithmetic and copies ran while one was open for 18% of the time, Pallas kernels for 0%

commit v1 on v0

v1 whole, which is shorter than its diff:
```python
import functools
import math

import jax
import jax.numpy as jnp
from jax import lax
from jax.experimental import pallas as pl
from jax.experimental.pallas import tpu as pltpu
from jax.sharding import PartitionSpec as P

ADAPTER_SCALING = 2.0
MESH = pl.DeviceIdType.MESH
F32 = jnp.float32
BF16 = jnp.bfloat16
LANES = 128


def iota(shape, dim):
    return lax.broadcasted_iota(jnp.int32, shape, dim)


def column(row, count, spread):
    shape = (count * spread, count)
    own = iota(shape, 0) // spread == iota(shape, 1)
    return jnp.sum(jnp.where(own, row.astype(F32), 0.0), axis=1, keepdims=True)


def kernel(
    n, nt, rank,
    lengths_ref, ids_ref, home_ref, new_key_ref, new_value_ref,
    queries_hbm, keys_hbm, values_hbm, w_hbm, a_hbm, up_hbm,
    out_ref,
    queries, keys, values, w, a, up,
    mixed_rows, att, positions, shrunk, base_send, base_recv, base_own, delta_send, delta_recv,
    load_q, load_k, load_v, load_w, load_a, load_up,
    pos_send, pos_recv, right_send, right_recv, left_send, left_recv,
    shrink_send, shrink_recv, bsend, brecv, dsend, drecv,
):
    rows, heads, width = queries.shape
    kv = keys.shape[0]
    per_kv = heads // kv
    feats = per_kv * width
    out_share = up.shape[1]
    stored = up.shape[0] // rank
    me = lax.axis_index("dp")
    mt = lax.axis_index("tensor")

    def block(t):
        return pl.ds(pl.multiple_of(t * out_share, out_share), out_share)

    get_q = pltpu.make_async_copy(queries_hbm, queries, load_q)
    get_q.start()
    get_k, get_v = [], []
    for c in range(kv):
        get_k.append(pltpu.make_async_copy(keys_hbm.at[:, c], keys.at[c], load_k.at[c]))
        get_v.append(pltpu.make_async_copy(values_hbm.at[:, c], values.at[c], load_v.at[c]))
        get_k[c].start()
        get_v[c].start()
    get_w = []
    for i in range(nt):
        t = lax.rem(mt + 1 + i, nt)
        get_w.append(pltpu.make_async_copy(w_hbm.at[:, block(t)], w.at[i], load_w.at[i]))
        get_w[i].start()
    get_a = pltpu.make_async_copy(a_hbm, a, load_a)
    get_a.start()
    get_up = pltpu.make_async_copy(up_hbm, up, load_up)
    get_up.start()

    barrier = pltpu.get_barrier_semaphore()
    for i in range(1, n):
        pl.semaphore_signal(barrier, inc=1, device_id={"dp": lax.rem(me + i, n)}, device_id_type=MESH)
    for i in range(1, nt):
        pl.semaphore_signal(barrier, inc=1, device_id={"tensor": lax.rem(mt + i, nt)}, device_id_type=MESH)

    adapters = home_ref.shape[1]
    id_column = column(ids_ref[...], rows, 1)
    match = id_column == iota((rows, adapters), 1).astype(F32)
    position = jnp.sum(jnp.where(match, home_ref[...].astype(F32), 0.0), axis=1, keepdims=True)
    positions[me] = jnp.broadcast_to(position, (rows, LANES))

    count = rows * per_kv
    visible_to = column(lengths_ref[...], rows, per_kv)
    visible = iota((count, keys.shape[2]), 1).astype(F32) < visible_to
    scale = 1.0 / math.sqrt(width)

    def line(c, source, step, to_right):
        send, recv = (right_send, right_recv) if to_right else (left_send, left_recv)
        return pltpu.make_async_remote_copy(
            src_ref=att.at[c, source], dst_ref=att.at[c, source],
            send_sem=send.at[c, step], recv_sem=recv.at[c, step],
            device_id={"dp": me + 1 if to_right else me - 1}, device_id_type=MESH,
        )

    def first_hop(c):
        @pl.when(me < n - 1)
        def _():
            line(c, me, 0, True).start()

        @pl.when(me > 0)
        def _():
            line(c, me, 0, False).start()

    def forward(c, hop):
        @pl.when(me >= hop)
        def _():
            line(c, me - hop, hop - 1, True).wait_recv()

            @pl.when(me < n - 1)
            def _():
                if hop < n - 1:
                    line(c, me - hop, hop, True).start()

        @pl.when(me + hop <= n - 1)
        def _():
            line(c, me + hop, hop - 1, False).wait_recv()

            @pl.when(me > 0)
            def _():
                if hop < n - 1:
                    line(c, me + hop, hop, False).start()

    def pos_copy(i):
        return pltpu.make_async_remote_copy(
            src_ref=positions.at[me], dst_ref=positions.at[me],
            send_sem=pos_send.at[i], recv_sem=pos_recv.at[i],
            device_id={"dp": lax.rem(me + i, n)}, device_id_type=MESH,
        )

    get_q.wait()
    for c in range(kv):
        q = queries[...]
        get_k[c].wait()
        scores = lax.dot_general(
            q, keys[c], (((2,), (2,)), ((0,), (0,))), preferred_element_type=F32
        )[:, c * per_kv:(c + 1) * per_kv, :].reshape(count, keys.shape[2]) * scale
        pick = (iota((count, rows * kv), 1) == (iota((count, rows * kv), 0) // per_kv) * kv + c).astype(BF16)
        own_key = jnp.dot(pick, new_key_ref[...], preferred_element_type=F32)
        own_value = jnp.dot(pick, new_value_ref[...], preferred_element_type=F32)
        qc = q.astype(F32)[:, c * per_kv:(c + 1) * per_kv, :].reshape(count, width)
        own = jnp.sum(qc * own_key, axis=1, keepdims=True) * scale
        top = jnp.maximum(jnp.max(jnp.where(visible, scores, -jnp.inf), axis=1, keepdims=True), own)
        weights = jnp.where(visible, jnp.exp(scores - top), 0.0)
        own_weight = jnp.exp(own - top)
        total = jnp.sum(weights, axis=1, keepdims=True) + own_weight
        probs = (weights / total).reshape(rows, per_kv, keys.shape[2]).astype(BF16)
        own_prob = (own_weight / total).astype(BF16).astype(F32)
        get_v[c].wait()
        mixed = lax.dot_general(
            probs, values[c], (((2,), (1,)), ((0,), (0,))), preferred_element_type=F32
        ).reshape(count, width)
        mixed_rows[...] = mixed + own_prob * own_value
        for g in range(per_kv):
            att[c, me, :, g * width:(g + 1) * width] = mixed_rows[pl.ds(g, rows, stride=per_kv), :].astype(BF16)
        if c == 0:
            pl.semaphore_wait(barrier, n - 1 + nt - 1)
            for i in range(1, n):
                pos_copy(i).start()
        first_hop(c)

    hops = [(c, hop) for hop in range(1, n) for c in range(kv)]
    per_step = -(-len(hops) // nt)

    def base_copy(i):
        return pltpu.make_async_remote_copy(
            src_ref=base_send.at[i], dst_ref=base_recv.at[i],
            send_sem=bsend.at[i], recv_sem=brecv.at[i],
            device_id={"tensor": lax.rem(mt + 1 + i, nt)}, device_id_type=MESH,
        )

    for i in range(nt):
        get_w[i].wait()
        partial = jnp.zeros((rows, out_share), F32)
        for c in range(kv):
            partial = partial + jnp.dot(
                att[c, me], w[i, c * feats:(c + 1) * feats, :], preferred_element_type=F32
            )
        if i < nt - 1:
            base_send[i] = partial.astype(BF16)
            base_copy(i).start()
        else:
            base_own[...] = partial
        for c, hop in hops[i * per_step:(i + 1) * per_step]:
            forward(c, hop)
    get_a.wait()
    for i in range(1, n):
        pos_copy(i).wait_recv()

    every = n * rows
    packs = LANES // rank
    half = iota((every, LANES), 1) // rank
    where = positions[...].reshape(every, LANES) - (me * stored).astype(F32)
    down = jnp.zeros((every, stored * rank), F32)
    for c in range(kv):
        down = down + lax.dot_general(
            att[c].reshape(every, feats), a[:, c * feats:(c + 1) * feats],
            (((1,), (1,)), ((), ())), preferred_element_type=F32,
        )
    folded = jnp.zeros((every, LANES), F32)
    for j in range(stored // packs):
        mine = where == (half + j * packs).astype(F32)
        folded = folded + jnp.where(mine, down[:, j * LANES:(j + 1) * LANES], 0.0)
    folded = folded + pltpu.roll(folded, rank, 1)
    short = every // 2
    low = iota((short, LANES), 1) < rank
    shrunk[0] = jnp.where(low, folded[:short], folded[short:]).astype(BF16)

    def shrink_copy(i):
        return pltpu.make_async_remote_copy(
            src_ref=shrunk.at[0], dst_ref=shrunk.at[i],
            send_sem=shrink_send.at[i], recv_sem=shrink_recv.at[i],
            device_id={"tensor": lax.rem(mt + i, nt)}, device_id_type=MESH,
        )

    for i in range(1, nt):
        shrink_copy(i).start()
    get_up.wait()
    total = shrunk[0].astype(F32)
    for i in range(1, nt):
        shrink_copy(i).wait_recv()
        total = total + shrunk[i].astype(F32)
    turned = pltpu.roll(total, rank, 1)
    whole = jnp.concatenate([jnp.where(low, total, turned), jnp.where(low, turned, total)], axis=0)
    spread = jnp.concatenate(
        [jnp.where(where == (half + j * packs).astype(F32), whole, 0.0) for j in range(stored // packs)], axis=1
    ).astype(BF16)

    delta = jnp.dot(spread, up[...], preferred_element_type=F32) * ADAPTER_SCALING
    delta_send[...] = delta.astype(BF16).reshape(n, rows, out_share)

    def delta_copy(i):
        to = lax.rem(me + i, n)
        return pltpu.make_async_remote_copy(
            src_ref=delta_send.at[to], dst_ref=delta_recv.at[i - 1],
            send_sem=dsend.at[i - 1], recv_sem=drecv.at[i - 1],
            device_id={"dp": to}, device_id_type=MESH,
        )

    for i in range(1, n):
        delta_copy(i).start()
    result = base_own[...] + delta_send[me].astype(F32)
    for i in range(nt - 1):
        base_copy(i).wait_recv()
        result = result + base_recv[i].astype(F32)
    for i in range(1, n):
        delta_copy(i).wait_recv()
        result = result + delta_recv[i - 1].astype(F32)
    out_ref[...] = result.astype(BF16)

    for i in range(1, n):
        pos_copy(i).wait_send()
        delta_copy(i).wait_send()
    for i in range(1, nt):
        shrink_copy(i).wait_send()
    for i in range(nt - 1):
        base_copy(i).wait_send()
    for c in range(kv):
        for step in range(n - 1):
            @pl.when((me < n - 1) & (me >= step))
            def _():
                line(c, me - step, step, True).wait_send()

            @pl.when((me > 0) & (me + step <= n - 1))
            def _():
                line(c, me + step, step, False).wait_send()


def local(
    n, nt,
    queries, cache_keys, cache_values, new_key, new_value, lengths,
    adapter_ids, adapter_home, w_out, factor_a, up_factor_table,
):
    rows, heads, width = queries.shape
    kv, span = cache_keys.shape[1:3]
    stored, rank, feats_all = factor_a.shape
    out_share = up_factor_table.shape[2]
    feats = feats_all // kv
    per_kv = heads // kv
    dma = pltpu.SemaphoreType.DMA
    vmem = pl.BlockSpec(memory_space=pltpu.VMEM)
    hbm = pl.BlockSpec(memory_space=pl.ANY)
    return pl.pallas_call(
        functools.partial(kernel, n, nt, rank),
        out_shape=jax.ShapeDtypeStruct((rows, out_share), BF16),
        in_specs=[vmem] * 5 + [hbm] * 6,
        out_specs=vmem,
        scratch_shapes=[
            pltpu.VMEM((rows, heads, width), BF16),
            pltpu.VMEM((kv, rows, span, width), BF16),
            pltpu.VMEM((kv, rows, span, width), BF16),
            pltpu.VMEM((nt, feats_all, out_share), BF16),
            pltpu.VMEM((stored * rank, feats_all), BF16),
            pltpu.VMEM((stored * rank, out_share), BF16),
            pltpu.VMEM((rows * per_kv, width), F32),
            pltpu.VMEM((kv, n, rows, feats), BF16),
            pltpu.VMEM((n, rows, LANES), F32),
            pltpu.VMEM((nt, n * rows // 2, LANES), BF16),
            pltpu.VMEM((nt - 1, rows, out_share), BF16),
            pltpu.VMEM((nt - 1, rows, out_share), BF16),
            pltpu.VMEM((rows, out_share), F32),
            pltpu.VMEM((n, rows, out_share), BF16),
            pltpu.VMEM((n - 1, rows, out_share), BF16),
            dma, dma((kv,)), dma((kv,)), dma((nt,)), dma, dma,
            dma((n,)), dma((n,)),
            dma((kv, n)), dma((kv, n)), dma((kv, n)), dma((kv, n)),
            dma((nt,)), dma((nt,)),
            dma((nt,)), dma((nt,)),
            dma((n,)), dma((n,)),
        ],
        compiler_params=pltpu.CompilerParams(
            collective_id=0, has_side_effects=True, vmem_limit_bytes=52 * 1024 * 1024
        ),
        name="attend_project",
    )(
        lengths, adapter_ids.reshape(1, rows), adapter_home.reshape(1, -1),
        new_key.reshape(rows * kv, width), new_value.reshape(rows * kv, width),
        queries, cache_keys, cache_values, w_out,
        factor_a.reshape(stored * rank, feats_all), up_factor_table.reshape(stored * rank, out_share),
    )


def solution(mesh):
    in_specs = (
        P(("parts", "dp"), "tensor", None),
        P(("parts", "dp"), "tensor", None, None),
        P(("parts", "dp"), "tensor", None, None),
        P(("parts", "dp"), "tensor", None),
        P(("parts", "dp"), "tensor", None),
        P(("parts", "dp"), None),
        P(("parts", "dp")),
        P("parts"),
        P("tensor", None),
        P("dp", None, "tensor"),
        P("dp", None, "tensor"),
    )
    out_specs = P(("parts", "dp"), "tensor")
    body = functools.partial(local, mesh.shape["dp"], mesh.shape["tensor"])
    return jax.shard_map(body, mesh=mesh, in_specs=in_specs, out_specs=out_specs, check_vma=False)
```

time: 124 us -> 37.9 us (0.31)
  waiting for transfers between devices: 46 us -> 0 us
  Pallas kernels: 0 us -> 31.4 us
  matrix products: 23.3 us -> 0 us
  blocking collectives: 20.3 us -> 0 us
  between operations: 14.3 us -> 0.02 us
  starting transfers between devices: 8.13 us -> 0 us
  other arithmetic: 2.95 us -> 0 us
  local copies, waits for them, and re-layouts: 8.13 us -> 6.16 us
    all_to_all x2 -> x0, waiting for transfers between devices: 36.8 us -> none  [the longest x1 36.8 us: local(): lax.all_to_all(packed_a, 'dp', split_axis=0, concat_axis=0, tiled=True)]
    pallas_call x0 -> x1, Pallas kernels: none -> 31.4 us  [local(): pl.pallas_call(functools.partial(kernel, n, nt, rank), out_shape=jax.Shap...]
    dot_general x9 -> x0, matrix products: 23.3 us -> none  [the longest x1 9.56 us: local(): base_output = jnp.dot(attended, w_out, preferred_element_type=jnp.float32)]
    psum x1 -> x0, blocking collectives: 10.4 us -> none  [local(): shrunk = lax.psum(shrink_part, 'tensor').astype(jnp.bfloat16)]
    unnamed x1 -> x0, blocking collectives: 9.89 us -> none
    reduce_scatter x1 -> x0, waiting for transfers between devices: 9.23 us -> none  [local(): lax.psum_scatter(base_output, 'tensor', scatter_dimension=1, tiled=True)]
    all_to_all x2 -> x0, starting transfers between devices: 8.09 us -> none  [the longest x1 4.57 us: local(): lax.all_to_all(packed_a, 'dp', split_axis=0, concat_axis=0, tiled=True)]
    convert_element_type x4 -> x0, local copies, waits for them, and re-layouts: 4.52 us -> none  [the longest x1 2.45 us: local(): packed_a = jnp.einsum('gsl,lkj->gskj', select, factor_a, preferred_elemen...]
  transfers between devices with their start and end apart: 3 -> 0, of which waited for: 2 -> 0; matrix products, arithmetic and copies ran while one was open for 18% -> 0% of each run, Pallas kernels for 0% -> 0%
where the time goes in v1:
time: 37.9 us; the launch traced here: 37.6 us
  Pallas kernels  31.4 us (83%)
  local copies, waits for them, and re-layouts  6.16 us (16%)
    pallas_call x1, Pallas kernels, local(): pl.pallas_call(functools.partial(kernel, n, nt, rank), out_shape=jax.Shap...  31.4 us
    unnamed x15, local copies, waits for them, and re-layouts  6.16 us

profile of v1, /device:TPU:0, one launch (start us, length us, event | category | flops | bytes accessed | tf_op | source)
XLA Modules:
  0.0 37.6 jit_solution(11373152953414897696)
XLA Ops:
  0.0 0.0 copy-start
  0.0 1.2 %copy-done = bf16[8,64,1024]{2,1,0:T(8,128)(2,1)S(1)} copy-done((bf16[8,64,1024]{2,1,0:T(8,128)(2,1)S(1)}, bf16[8,64,1024]{2,1,0:T(8,128)(2,1)}, u32[]{:S(2)}) %copy-start) | copy-done | bytes 1048600
  1.2 0.0 copy-start.1
  1.2 0.9 %copy-done.1 = bf16[32,16,128]{2,1,0:T(8,128)(2,1)S(1)} copy-done((bf16[32,16,128]{2,1,0:T(8,128)(2,1)S(1)}, bf16[32,16,128]{2,1,0:T(8,128)(2,1)}, u32[]{:S(2)}) %copy-start.1) | copy-done | bytes 131096
  2.1 0.0 copy-start.2
  2.1 0.7 %copy-done.2 = bf16[32,2,128]{2,1,0:T(2,128)(2,1)S(1)} copy-done((bf16[32,2,128]{2,1,0:T(2,128)(2,1)S(1)}, bf16[32,2,128]{2,1,0:T(2,128)(2,1)}, u32[]{:S(2)}) %copy-start.2) | copy-done | bytes 16408
  2.8 0.0 copy-start.3
  2.9 0.7 %copy-done.3 = bf16[32,2,128]{2,1,0:T(2,128)(2,1)S(1)} copy-done((bf16[32,2,128]{2,1,0:T(2,128)(2,1)S(1)}, bf16[32,2,128]{2,1,0:T(2,128)(2,1)}, u32[]{:S(2)}) %copy-start.3) | copy-done | bytes 16408
  3.6 0.0 copy-start.4
  3.6 0.7 %copy-done.4 = s32[1,32]{1,0:T(1,128)S(1)} copy-done((s32[1,32]{1,0:T(1,128)S(1)}, s32[1,32]{1,0:T(1,128)}, u32[]{:S(2)}) %copy-start.4) | copy-done | bytes 152
  4.2 0.0 copy-start.5
  4.2 0.7 %copy-done.5 = s32[32]{0:T(128)S(1)} copy-done((s32[32]{0:T(128)S(1)}, s32[32]{0:T(128)}, u32[]{:S(2)}) %copy-start.5) | copy-done | bytes 152
  4.9 0.0 copy-start.6
  4.9 0.7 %copy-done.6 = s32[32]{0:T(128)S(1)} copy-done((s32[32]{0:T(128)S(1)}, s32[32]{0:T(128)}, u32[]{:S(2)}) %copy-start.6) | copy-done | bytes 152
  5.5 31.4 %attend_project.1 = bf16[32,1024]{1,0:T(8,128)(2,1)S(1)} custom-call(s32[1,32]{1,0:T(1,128)S(1)} %copy-done.4, s32[1,32]{1,0:T(1,128)S(1)} %bitcast.9, s32[1,32]{1,0:T(1,128)S(1)} %bitcast.10, bf16[64,128]{1,0:T(8,128)(2,1)S(1)} %bitcast.7, bf16[64,128]{1,0:T(8,128)(2,1)S(1)} %bitcast.8, bf16[32,16,128]{2,1,0:T(8,128)(2,1)S(1)} %copy-done.1, ...), custom_call_target="tpu_custom_call" | custom-call | tf_op jit(solution)/shard_map/attend_project/pallas_call | solution.py:281
  36.9 0.6 %copy.13 = bf16[32,1024]{1,0:T(8,128)(2,1)} copy(bf16[32,1024]{1,0:T(8,128)(2,1)S(1)} %attend_project.1) | data formatting | bytes 131072
Async XLA Ops:
  0.0 1.2 %copy-start = (bf16[8,64,1024]{2,1,0:T(8,128)(2,1)S(1)}, bf16[8,64,1024]{2,1,0:T(8,128)(2,1)}, u32[]{:S(2)}) copy-start(bf16[8,64,1024]{2,1,0:T(8,128)(2,1)} %param.21) | copy-start | bytes 3145732
  1.2 0.9 %copy-start.1 = (bf16[32,16,128]{2,1,0:T(8,128)(2,1)S(1)}, bf16[32,16,128]{2,1,0:T(8,128)(2,1)}, u32[]{:S(2)}) copy-start(bf16[32,16,128]{2,1,0:T(8,128)(2,1)} %queries_hbm.1) | copy-start | bytes 393220
  2.1 0.7 %copy-start.2 = (bf16[32,2,128]{2,1,0:T(2,128)(2,1)S(1)}, bf16[32,2,128]{2,1,0:T(2,128)(2,1)}, u32[]{:S(2)}) copy-start(bf16[32,2,128]{2,1,0:T(2,128)(2,1)} %param.14) | copy-start | bytes 49156
  2.8 0.7 %copy-start.3 = (bf16[32,2,128]{2,1,0:T(2,128)(2,1)S(1)}, bf16[32,2,128]{2,1,0:T(2,128)(2,1)}, u32[]{:S(2)}) copy-start(bf16[32,2,128]{2,1,0:T(2,128)(2,1)} %param.15) | copy-start | bytes 49156
  3.6 0.7 %copy-start.4 = (s32[1,32]{1,0:T(1,128)S(1)}, s32[1,32]{1,0:T(1,128)}, u32[]{:S(2)}) copy-start(s32[1,32]{1,0:T(1,128)} %lengths_ref.1) | copy-start | bytes 388
  4.2 0.7 %copy-start.5 = (s32[32]{0:T(128)S(1)}, s32[32]{0:T(128)}, u32[]{:S(2)}) copy-start(s32[32]{0:T(128)} %param.17) | copy-start | bytes 388
  4.9 0.7 %copy-start.6 = (s32[32]{0:T(128)S(1)}, s32[32]{0:T(128)}, u32[]{:S(2)}) copy-start(s32[32]{0:T(128)} %param.18) | copy-start | bytes 388

commit v2 on v1

v2 whole, which is shorter than its diff:
```python
import functools
import math

import jax
import jax.numpy as jnp
from jax import lax
from jax.experimental import pallas as pl
from jax.experimental.pallas import tpu as pltpu
from jax.sharding import PartitionSpec as P

ADAPTER_SCALING = 2.0
MESH = pl.DeviceIdType.MESH
F32 = jnp.float32
BF16 = jnp.bfloat16
LANES = 128
HALVES = 1
GREETED = 0
STRIDES = (1, 1)


def iota(shape, dim):
    return lax.broadcasted_iota(jnp.int32, shape, dim)


def stride(j):
    return STRIDES[min(j, len(STRIDES) - 1)]


def column(row, count, spread):
    shape = (count * spread, count)
    own = iota(shape, 0) // spread == iota(shape, 1)
    return jnp.sum(jnp.where(own, row.astype(F32), 0.0), axis=1, keepdims=True)


def kernel(
    n, nt, rank,
    lengths_hbm, ids_hbm, home_hbm, new_key_hbm, new_value_hbm,
    queries_hbm, keys_hbm, values_hbm, w_hbm, a_hbm, up_hbm,
    out_ref,
    lengths, ids, home, new_key, new_value,
    queries, keys, values, w, a, up,
    mixed_rows, own_att, att, positions, shrunk, base_send, base_recv, base_own, delta_send, delta_recv,
    load_small, load_q, load_k, load_v, load_w, load_a, load_up,
    pos_send, pos_recv, right_send, right_recv, left_send, left_recv,
    shrink_send, shrink_recv, bsend, brecv, dsend, drecv,
):
    rows, heads, width = queries.shape
    kv, span = keys.shape[0], keys.shape[2]
    per_kv = heads // kv
    feats = per_kv * width
    out_share = up.shape[1]
    stored = up.shape[0] // rank
    part = rows // HALVES
    me = lax.axis_index("dp")
    mt = lax.axis_index("tensor")

    def block(t):
        return pl.ds(pl.multiple_of(t * out_share, out_share), out_share)

    small = [(ids_hbm, ids), (home_hbm, home), (lengths_hbm, lengths), (new_key_hbm, new_key), (new_value_hbm, new_value)]
    get_small = [pltpu.make_async_copy(x, y, load_small.at[i]) for i, (x, y) in enumerate(small)]
    for get in get_small:
        get.start()
    get_q = pltpu.make_async_copy(queries_hbm, queries, load_q)
    get_q.start()
    chunks = [(h, k) for h in range(HALVES) for k in range(kv)]
    get_k, get_v = [], []
    for j, (h, k) in enumerate(chunks):
        here = pl.ds(h * part, part)
        get_k.append(pltpu.make_async_copy(keys_hbm.at[here, k], keys.at[k, here], load_k.at[j]))
        get_v.append(pltpu.make_async_copy(values_hbm.at[here, k], values.at[k, here], load_v.at[j]))
        get_k[j].start()
        get_v[j].start()
    get_w = []
    for i in range(nt):
        t = lax.rem(mt + 1 + i, nt)
        get_w.append(pltpu.make_async_copy(w_hbm.at[:, block(t)], w.at[i], load_w.at[i]))
    get_a = pltpu.make_async_copy(a_hbm, a, load_a)
    get_up = pltpu.make_async_copy(up_hbm, up, load_up)

    barrier = pltpu.get_barrier_semaphore()
    for i in range(1, n):
        pl.semaphore_signal(barrier, inc=1, device_id={"dp": lax.rem(me + i, n)}, device_id_type=MESH)
    for i in range(1, nt):
        pl.semaphore_signal(barrier, inc=1, device_id={"tensor": lax.rem(mt + i, nt)}, device_id_type=MESH)

    for get in get_small:
        get.wait()
    adapters = home.shape[1]
    id_column = column(ids[...], rows, 1)
    match = id_column == iota((rows, adapters), 1).astype(F32)
    position = jnp.sum(jnp.where(match, home[...].astype(F32), 0.0), axis=1, keepdims=True)
    positions[me] = jnp.broadcast_to(position, (rows, LANES))

    def line(j, slot, distance, step, sign):
        send, recv = (right_send, right_recv) if sign > 0 else (left_send, left_recv)
        return pltpu.make_async_remote_copy(
            src_ref=att.at[j, slot], dst_ref=att.at[j, slot],
            send_sem=send.at[j, distance], recv_sem=recv.at[j, distance],
            device_id={"dp": me + sign * step}, device_id_type=MESH,
        )

    def reaches(offset):
        return (me + offset >= 0) & (me + offset <= n - 1)

    def pass_on(j, source, act):
        for step in range(min(stride(j), n - 1), 0, -1):
            for sign in (1, -1):
                if source + step < n:
                    @pl.when(reaches(sign * step) & reaches(-sign * source))
                    def _():
                        act(line(j, me - sign * source, source + step, step, sign))

    def arrive(j, distance):
        for sign in (1, -1):
            @pl.when(reaches(-sign * distance))
            def _():
                came = (distance - 1) % stride(j) + 1
                line(j, me - sign * distance, distance, came, sign).wait_recv()
        if distance % stride(j) == 0:
            pass_on(j, distance, lambda copy: copy.start())

    def pos_copy(i):
        return pltpu.make_async_remote_copy(
            src_ref=positions.at[me], dst_ref=positions.at[me],
            send_sem=pos_send.at[i], recv_sem=pos_recv.at[i],
            device_id={"dp": lax.rem(me + i, n)}, device_id_type=MESH,
        )

    def base_copy(i):
        return pltpu.make_async_remote_copy(
            src_ref=base_send.at[i], dst_ref=base_recv.at[i],
            send_sem=bsend.at[i], recv_sem=brecv.at[i],
            device_id={"tensor": lax.rem(mt + 1 + i, nt)}, device_id_type=MESH,
        )

    def shrink_copy(h, i):
        return pltpu.make_async_remote_copy(
            src_ref=shrunk.at[h, 0], dst_ref=shrunk.at[h, i],
            send_sem=shrink_send.at[h, i], recv_sem=shrink_recv.at[h, i],
            device_id={"tensor": lax.rem(mt + i, nt)}, device_id_type=MESH,
        )

    def delta_copy(h, i):
        to = lax.rem(me + i, n)
        return pltpu.make_async_remote_copy(
            src_ref=delta_send.at[h, to], dst_ref=delta_recv.at[h, i - 1],
            send_sem=dsend.at[h, i - 1], recv_sem=drecv.at[h, i - 1],
            device_id={"dp": to}, device_id_type=MESH,
        )

    count = part * per_kv
    scale = 1.0 / math.sqrt(width)
    reach = column(lengths[...], rows, per_kv)
    get_q.wait()
    for j, (h, k) in enumerate(chunks):
        visible = iota((count, span), 1).astype(F32) < reach[h * count:(h + 1) * count]
        q = queries[h * part:(h + 1) * part]
        get_k[j].wait()
        scores = lax.dot_general(
            q, keys[k, h * part:(h + 1) * part], (((2,), (2,)), ((0,), (0,))), preferred_element_type=F32
        )[:, k * per_kv:(k + 1) * per_kv, :].reshape(count, span) * scale
        row = iota((count, rows * kv), 0) // per_kv + h * part
        pick = (iota((count, rows * kv), 1) == row * kv + k).astype(BF16)
        own_key = jnp.dot(pick, new_key[...], preferred_element_type=F32)
        own_value = jnp.dot(pick, new_value[...], preferred_element_type=F32)
        qk = q.astype(F32)[:, k * per_kv:(k + 1) * per_kv, :].reshape(count, width)
        own = jnp.sum(qk * own_key, axis=1, keepdims=True) * scale
        top = jnp.maximum(jnp.max(jnp.where(visible, scores, -jnp.inf), axis=1, keepdims=True), own)
        weights = jnp.where(visible, jnp.exp(scores - top), 0.0)
        own_weight = jnp.exp(own - top)
        total = jnp.sum(weights, axis=1, keepdims=True) + own_weight
        probs = (weights / total).reshape(part, per_kv, span).astype(BF16)
        own_prob = (own_weight / total).astype(BF16).astype(F32)
        get_v[j].wait()
        mixed = lax.dot_general(
            probs, values[k, h * part:(h + 1) * part], (((2,), (1,)), ((0,), (0,))), preferred_element_type=F32
        ).reshape(count, width)
        mixed_rows[...] = mixed + own_prob * own_value
        for g in range(per_kv):
            piece = mixed_rows[pl.ds(g, part, stride=per_kv), :].astype(BF16)
            att[j, me, :, g * width:(g + 1) * width] = piece
            own_att[h * part:(h + 1) * part, k * feats + g * width:k * feats + (g + 1) * width] = piece
        if j == 0:
            get_a.start()
            for get in get_w:
                get.start()
            get_up.start()
        if j == GREETED:
            pl.semaphore_wait(barrier, n - 1 + nt - 1)
            for i in range(1, n):
                pos_copy(i).start()
            for i in range(j):
                pass_on(i, 0, lambda copy: copy.start())
        if j >= GREETED:
            pass_on(j, 0, lambda copy: copy.start())

    def base(i):
        get_w[i].wait()
        partial = jnp.dot(own_att[...], w[i], preferred_element_type=F32)
        if i < nt - 1:
            base_send[i] = partial.astype(BF16)
            base_copy(i).start()
        else:
            base_own[...] = partial

    every = n * part
    short = every // 2
    packs = LANES // rank
    half = iota((every, LANES), 1) // rank
    low = iota((short, LANES), 1) < rank

    def keeps(h, j):
        where = positions[:, h * part:(h + 1) * part, :].reshape(every, LANES) - (me * stored).astype(F32)
        return where == (half + j * packs).astype(F32)

    def shrink(h):
        if h == 0:
            get_a.wait()
            for i in range(1, n):
                pos_copy(i).wait_recv()
        down = jnp.zeros((every, stored * rank), F32)
        for k in range(kv):
            down = down + lax.dot_general(
                att[h * kv + k].reshape(every, feats), a[:, k * feats:(k + 1) * feats],
                (((1,), (1,)), ((), ())), preferred_element_type=F32,
            )
        folded = jnp.zeros((every, LANES), F32)
        for j in range(stored // packs):
            folded = folded + jnp.where(keeps(h, j), down[:, j * LANES:(j + 1) * LANES], 0.0)
        folded = folded + pltpu.roll(folded, rank, 1)
        shrunk[h, 0] = jnp.where(low, folded[:short], folded[short:]).astype(BF16)
        for i in range(1, nt):
            shrink_copy(h, i).start()

    def expand(h):
        if h == 0:
            get_up.wait()
        total = shrunk[h, 0].astype(F32)
        for i in range(1, nt):
            shrink_copy(h, i).wait_recv()
            total = total + shrunk[h, i].astype(F32)
        turned = pltpu.roll(total, rank, 1)
        whole = jnp.concatenate([jnp.where(low, total, turned), jnp.where(low, turned, total)], axis=0)
        spread = jnp.concatenate(
            [jnp.where(keeps(h, j), whole, 0.0) for j in range(stored // packs)], axis=1
        ).astype(BF16)
        delta = jnp.dot(spread, up[...], preferred_element_type=F32) * ADAPTER_SCALING
        delta_send[h] = delta.astype(BF16).reshape(n, part, out_share)
        for i in range(1, n):
            delta_copy(h, i).start()

    events = sorted(
        ((j, d) for j in range(len(chunks)) for d in range(1, n)),
        key=lambda e: (e[0] + 3 * ((e[1] - 1) // stride(e[0])), -e[1]),
    )
    bases = list(range(nt))
    last = {h: max(i for i, (j, d) in enumerate(events) if chunks[j][0] == h) for h in range(HALVES)}
    for at, (j, d) in enumerate(events):
        handed = d % stride(j) == 0 and d < n - 1
        if not handed:
            while len(bases) > 1 and not any(e[1] % stride(e[0]) == 0 and e[1] < n - 1 for e in events[at:]):
                base(bases.pop(0))
        arrive(j, d)
        if handed and len(bases) > 1:
            base(bases.pop(0))
        for h in range(HALVES):
            if last[h] == at:
                shrink(h)
    for i in bases:
        base(i)
    for h in range(HALVES):
        expand(h)

    for h in range(HALVES):
        here = slice(h * part, (h + 1) * part)
        result = base_own[here] + delta_send[h, me].astype(F32)
        for i in range(nt - 1):
            if h == 0:
                base_copy(i).wait_recv()
            result = result + base_recv[i, here].astype(F32)
        for i in range(1, n):
            delta_copy(h, i).wait_recv()
            result = result + delta_recv[h, i - 1].astype(F32)
        out_ref[here] = result.astype(BF16)

    for i in range(1, n):
        pos_copy(i).wait_send()
        for h in range(HALVES):
            delta_copy(h, i).wait_send()
    for i in range(1, nt):
        for h in range(HALVES):
            shrink_copy(h, i).wait_send()
    for i in range(nt - 1):
        base_copy(i).wait_send()
    for j in range(len(chunks)):
        for source in range(0, n, stride(j)):
            pass_on(j, source, lambda copy: copy.wait_send())


def local(
    n, nt,
    queries, cache_keys, cache_values, new_key, new_value, lengths,
    adapter_ids, adapter_home, w_out, factor_a, up_factor_table,
):
    rows, heads, width = queries.shape
    kv, span = cache_keys.shape[1:3]
    stored, rank, feats_all = factor_a.shape
    out_share = up_factor_table.shape[2]
    feats = feats_all // kv
    per_kv = heads // kv
    dma = pltpu.SemaphoreType.DMA
    vmem = pl.BlockSpec(memory_space=pltpu.VMEM)
    hbm = pl.BlockSpec(memory_space=pltpu.HBM)
    chunks = HALVES * kv
    part = rows // HALVES
    return pl.pallas_call(
        functools.partial(kernel, n, nt, rank),
        out_shape=jax.ShapeDtypeStruct((rows, out_share), BF16),
        in_specs=[hbm] * 11,
        out_specs=vmem,
        scratch_shapes=[
            pltpu.VMEM((1, rows), jnp.int32),
            pltpu.VMEM((1, rows), jnp.int32),
            pltpu.VMEM((1, adapter_home.shape[0]), jnp.int32),
            pltpu.VMEM((rows * kv, width), BF16),
            pltpu.VMEM((rows * kv, width), BF16),
            pltpu.VMEM((rows, heads, width), BF16),
            pltpu.VMEM((kv, rows, span, width), BF16),
            pltpu.VMEM((kv, rows, span, width), BF16),
            pltpu.VMEM((nt, feats_all, out_share), BF16),
            pltpu.VMEM((stored * rank, feats_all), BF16),
            pltpu.VMEM((stored * rank, out_share), BF16),
            pltpu.VMEM((part * per_kv, width), F32),
            pltpu.VMEM((rows, feats_all), BF16),
            pltpu.VMEM((chunks, n, part, feats), BF16),
            pltpu.VMEM((n, rows, LANES), F32),
            pltpu.VMEM((HALVES, nt, n * part // 2, LANES), BF16),
            pltpu.VMEM((nt - 1, rows, out_share), BF16),
            pltpu.VMEM((nt - 1, rows, out_share), BF16),
            pltpu.VMEM((rows, out_share), F32),
            pltpu.VMEM((HALVES, n, part, out_share), BF16),
            pltpu.VMEM((HALVES, n - 1, part, out_share), BF16),
            dma((5,)), dma, dma((chunks,)), dma((chunks,)), dma((nt,)), dma, dma,
            dma((n,)), dma((n,)),
            dma((chunks, n)), dma((chunks, n)), dma((chunks, n)), dma((chunks, n)),
            dma((HALVES, nt)), dma((HALVES, nt)),
            dma((nt,)), dma((nt,)),
            dma((HALVES, n)), dma((HALVES, n)),
        ],
        compiler_params=pltpu.CompilerParams(
            collective_id=0, has_side_effects=True, vmem_limit_bytes=60 * 1024 * 1024
        ),
        name="attend_project",
    )(
        lengths, adapter_ids.reshape(1, rows), adapter_home.reshape(1, -1),
        new_key.reshape(rows * kv, width), new_value.reshape(rows * kv, width),
        queries, cache_keys, cache_values, w_out,
        factor_a.reshape(stored * rank, feats_all), up_factor_table.reshape(stored * rank, out_share),
    )


def solution(mesh):
    in_specs = (
        P(("parts", "dp"), "tensor", None),
        P(("parts", "dp"), "tensor", None, None),
        P(("parts", "dp"), "tensor", None, None),
        P(("parts", "dp"), "tensor", None),
        P(("parts", "dp"), "tensor", None),
        P(("parts", "dp"), None),
        P(("parts", "dp")),
        P("parts"),
        P("tensor", None),
        P("dp", None, "tensor"),
        P("dp", None, "tensor"),
    )
    out_specs = P(("parts", "dp"), "tensor")
    body = functools.partial(local, mesh.shape["dp"], mesh.shape["tensor"])
    return jax.shard_map(body, mesh=mesh, in_specs=in_specs, out_specs=out_specs, check_vma=False)
```

time: 37.9 us -> 30.6 us (0.81)
  local copies, waits for them, and re-layouts: 6.16 us -> 1.47 us
  Pallas kernels: 31.4 us -> 28.9 us
    unnamed x15 -> x1, local copies, waits for them, and re-layouts: 6.16 us -> 1.47 us
    pallas_call x1, Pallas kernels: 31.4 us -> 28.9 us  [local(): pl.pallas_call(functools.partial(kernel, n, nt, rank), out_shape=jax.Shap...]
where the time goes in v2:
time: 30.6 us; the launch traced here: 30.4 us
  Pallas kernels  28.9 us (94%)
  local copies, waits for them, and re-layouts  1.47 us (5%)
    pallas_call x1, Pallas kernels, local(): pl.pallas_call(functools.partial(kernel, n, nt, rank), out_shape=jax.Shap...  28.9 us
    unnamed x1, local copies, waits for them, and re-layouts  1.47 us

profile of v2, /device:TPU:0, one launch (start us, length us, event | category | flops | bytes accessed | tf_op | source)
XLA Modules:
  0.0 30.4 jit_solution(2086657274844874068)
XLA Ops:
  0.0 28.9 %attend_project.1 = bf16[32,1024]{1,0:T(8,128)(2,1)} custom-call(s32[1,32]{1,0:T(1,128)} %lengths_hbm.1, s32[1,32]{1,0:T(1,128)} %bitcast.10, s32[1,32]{1,0:T(1,128)} %bitcast.11, bf16[64,128]{1,0:T(8,128)(2,1)} %bitcast.8, bf16[64,128]{1,0:T(8,128)(2,1)} %bitcast.9, bf16[32,16,128]{2,1,0:T(8,128)(2,1)} %queries_hbm.1, bf16[32,2,128,128]{3,2,1,0:T(8,128)(2,1)} %keys_hbm.1, ...), custom_call_target="tpu_custom_call" | custom-call | tf_op jit(solution)/shard_map/attend_project/pallas_call | solution.py:317
  28.9 1.5 %copy.13 = bf16[32,1024]{1,0:T(8,128)(2,1)} copy(bf16[32,1024]{1,0:T(8,128)(2,1)} %attend_project.1) | data formatting | bytes 131072

commit v3 on v2

--- a/solution.py
+++ b/solution.py
@@ -14,7 +14,6 @@
 BF16 = jnp.bfloat16
 LANES = 128
 HALVES = 1
-GREETED = 0
 STRIDES = (1, 1)
 
 
@@ -41,7 +40,7 @@
     queries, keys, values, w, a, up,
     mixed_rows, own_att, att, positions, shrunk, base_send, base_recv, base_own, delta_send, delta_recv,
     load_small, load_q, load_k, load_v, load_w, load_a, load_up,
-    pos_send, pos_recv, right_send, right_recv, left_send, left_recv,
+    right_send, right_recv, left_send, left_recv,
     shrink_send, shrink_recv, bsend, brecv, dsend, drecv,
 ):
     rows, heads, width = queries.shape
@@ -69,8 +68,9 @@
         here = pl.ds(h * part, part)
         get_k.append(pltpu.make_async_copy(keys_hbm.at[here, k], keys.at[k, here], load_k.at[j]))
         get_v.append(pltpu.make_async_copy(values_hbm.at[here, k], values.at[k, here], load_v.at[j]))
-        get_k[j].start()
-        get_v[j].start()
+        if j == 0:
+            get_k[j].start()
+            get_v[j].start()
     get_w = []
     for i in range(nt):
         t = lax.rem(mt + 1 + i, nt)
@@ -86,16 +86,11 @@
 
     for get in get_small:
         get.wait()
-    adapters = home.shape[1]
-    id_column = column(ids[...], rows, 1)
-    match = id_column == iota((rows, adapters), 1).astype(F32)
-    position = jnp.sum(jnp.where(match, home[...].astype(F32), 0.0), axis=1, keepdims=True)
-    positions[me] = jnp.broadcast_to(position, (rows, LANES))
-
     def line(j, slot, distance, step, sign):
         send, recv = (right_send, right_recv) if sign > 0 else (left_send, left_recv)
+        piece = positions.at[slot] if j == len(chunks) else att.at[j, slot]
         return pltpu.make_async_remote_copy(
-            src_ref=att.at[j, slot], dst_ref=att.at[j, slot],
+            src_ref=piece, dst_ref=piece,
             send_sem=send.at[j, distance], recv_sem=recv.at[j, distance],
             device_id={"dp": me + sign * step}, device_id_type=MESH,
         )
@@ -120,13 +115,6 @@
         if distance % stride(j) == 0:
             pass_on(j, distance, lambda copy: copy.start())
 
-    def pos_copy(i):
-        return pltpu.make_async_remote_copy(
-            src_ref=positions.at[me], dst_ref=positions.at[me],
-            send_sem=pos_send.at[i], recv_sem=pos_recv.at[i],
-            device_id={"dp": lax.rem(me + i, n)}, device_id_type=MESH,
-        )
-
     def base_copy(i):
         return pltpu.make_async_remote_copy(
             src_ref=base_send.at[i], dst_ref=base_recv.at[i],
@@ -157,6 +145,9 @@
         visible = iota((count, span), 1).astype(F32) < reach[h * count:(h + 1) * count]
         q = queries[h * part:(h + 1) * part]
         get_k[j].wait()
+        if j + 1 < len(chunks):
+            get_k[j + 1].start()
+            get_v[j + 1].start()
         scores = lax.dot_general(
             q, keys[k, h * part:(h + 1) * part], (((2,), (2,)), ((0,), (0,))), preferred_element_type=F32
         )[:, k * per_kv:(k + 1) * per_kv, :].reshape(count, span) * scale
@@ -186,14 +177,15 @@
             for get in get_w:
                 get.start()
             get_up.start()
-        if j == GREETED:
             pl.semaphore_wait(barrier, n - 1 + nt - 1)
-            for i in range(1, n):
-                pos_copy(i).start()
-            for i in range(j):
-                pass_on(i, 0, lambda copy: copy.start())
-        if j >= GREETED:
-            pass_on(j, 0, lambda copy: copy.start())
+        pass_on(j, 0, lambda copy: copy.start())
+        if j == 0:
+            adapters = home.shape[1]
+            id_column = column(ids[...], rows, 1)
+            match = id_column == iota((rows, adapters), 1).astype(F32)
+            position = jnp.sum(jnp.where(match, home[...].astype(F32), 0.0), axis=1, keepdims=True)
+            positions[me] = jnp.broadcast_to(position, (rows, LANES))
+            pass_on(len(chunks), 0, lambda copy: copy.start())
 
     def base(i):
         get_w[i].wait()
@@ -217,8 +209,6 @@
     def shrink(h):
         if h == 0:
             get_a.wait()
-            for i in range(1, n):
-                pos_copy(i).wait_recv()
         down = jnp.zeros((every, stored * rank), F32)
         for k in range(kv):
             down = down + lax.dot_general(
@@ -247,22 +237,22 @@
         ).astype(BF16)
         delta = jnp.dot(spread, up[...], preferred_element_type=F32) * ADAPTER_SCALING
         delta_send[h] = delta.astype(BF16).reshape(n, part, out_share)
-        for i in range(1, n):
+        for i in sorted(range(1, n), key=lambda i: min(i, n - i)):
             delta_copy(h, i).start()
 
     events = sorted(
-        ((j, d) for j in range(len(chunks)) for d in range(1, n)),
-        key=lambda e: (e[0] + 3 * ((e[1] - 1) // stride(e[0])), -e[1]),
+        ((j, d) for j in range(len(chunks) + 1) for d in range(1, n)),
+        key=lambda e: ((e[0] if e[0] < len(chunks) else 0.5) + 3 * ((e[1] - 1) // stride(e[0])), -e[1]),
     )
     bases = list(range(nt))
-    last = {h: max(i for i, (j, d) in enumerate(events) if chunks[j][0] == h) for h in range(HALVES)}
+    last = {h: max(i for i, (j, d) in enumerate(events) if j < len(chunks) and chunks[j][0] == h) for h in range(HALVES)}
     for at, (j, d) in enumerate(events):
         handed = d % stride(j) == 0 and d < n - 1
         if not handed:
             while len(bases) > 1 and not any(e[1] % stride(e[0]) == 0 and e[1] < n - 1 for e in events[at:]):
                 base(bases.pop(0))
         arrive(j, d)
-        if handed and len(bases) > 1:
+        if handed and j < len(chunks) and len(bases) > 1:
             base(bases.pop(0))
         for h in range(HALVES):
             if last[h] == at:
@@ -285,7 +275,6 @@
         out_ref[here] = result.astype(BF16)
 
     for i in range(1, n):
-        pos_copy(i).wait_send()
         for h in range(HALVES):
             delta_copy(h, i).wait_send()
     for i in range(1, nt):
@@ -293,7 +282,7 @@
             shrink_copy(h, i).wait_send()
     for i in range(nt - 1):
         base_copy(i).wait_send()
-    for j in range(len(chunks)):
+    for j in range(len(chunks) + 1):
         for source in range(0, n, stride(j)):
             pass_on(j, source, lambda copy: copy.wait_send())
 
@@ -342,8 +331,7 @@
             pltpu.VMEM((HALVES, n, part, out_share), BF16),
             pltpu.VMEM((HALVES, n - 1, part, out_share), BF16),
             dma((5,)), dma, dma((chunks,)), dma((chunks,)), dma((nt,)), dma, dma,
-            dma((n,)), dma((n,)),
-            dma((chunks, n)), dma((chunks, n)), dma((chunks, n)), dma((chunks, n)),
+            dma((chunks + 1, n)), dma((chunks + 1, n)), dma((chunks + 1, n)), dma((chunks + 1, n)),
             dma((HALVES, nt)), dma((HALVES, nt)),
             dma((nt,)), dma((nt,)),
             dma((HALVES, n)), dma((HALVES, n)),

time: 30.6 us -> 30.2 us (0.987)
  Pallas kernels: 28.9 us -> 28.5 us
    pallas_call x1, Pallas kernels: 28.9 us -> 28.5 us  [local(): pl.pallas_call(functools.partial(kernel, n, nt, rank), out_shape=jax.Shap...]
where the time goes in v3:
time: 30.2 us; the launch traced here: 30 us
  Pallas kernels  28.5 us (94%)
  local copies, waits for them, and re-layouts  1.47 us (5%)
    pallas_call x1, Pallas kernels, local(): pl.pallas_call(functools.partial(kernel, n, nt, rank), out_shape=jax.Shap...  28.5 us
    unnamed x1, local copies, waits for them, and re-layouts  1.47 us

profile of v3, /device:TPU:0, one launch (start us, length us, event | category | flops | bytes accessed | tf_op | source)
XLA Modules:
  0.0 30.0 jit_solution(7288217543709930539)
XLA Ops:
  0.0 28.5 %attend_project.1 = bf16[32,1024]{1,0:T(8,128)(2,1)} custom-call(s32[1,32]{1,0:T(1,128)} %lengths_hbm.1, s32[1,32]{1,0:T(1,128)} %bitcast.10, s32[1,32]{1,0:T(1,128)} %bitcast.11, bf16[64,128]{1,0:T(8,128)(2,1)} %bitcast.8, bf16[64,128]{1,0:T(8,128)(2,1)} %bitcast.9, bf16[32,16,128]{2,1,0:T(8,128)(2,1)} %queries_hbm.1, bf16[32,2,128,128]{3,2,1,0:T(8,128)(2,1)} %keys_hbm.1, ...), custom_call_target="tpu_custom_call" | custom-call | tf_op jit(solution)/shard_map/attend_project/pallas_call | solution.py:306
  28.5 1.5 %copy.13 = bf16[32,1024]{1,0:T(8,128)(2,1)} copy(bf16[32,1024]{1,0:T(8,128)(2,1)} %attend_project.1) | data formatting | bytes 131072
